TPU v7x, 256 devices: a whole 4x4x8 slice. The times are simulated.
256 devices in a mesh: blk: 64 (over y, x_lo, z), rep: 4 (over x_hi, core).
Axes of the slice: x: 4 (x_hi: 2, x_lo: 2; x = x_hi * 2 + x_lo), y: 4, z: 8, core: 2. Of those that a mesh axis runs over, the one named last changes fastest.
Arguments:
- image_feats: bfloat16 [131072, 1152], P(('blk', 'rep')), may hold values from -16 to 16, as said below
- text_feats: bfloat16 [131072, 1152], P(('blk', 'rep')), may hold values from -16 to 16, as said below
- head: bfloat16 [1152, 1152], replicated, may hold values from -0.1875 to 0.1875
- image_ids: int32 [131072], P(('blk', 'rep')), may hold values from 0 to 2047
- text_ids: int32 [131072], P(('blk', 'rep')), may hold values from 0 to 2047
- log_scale: float32 [1], replicated, may hold values from 3 to 3.7
- bias: float32 [1], replicated, may hold values from -3 to -1
Outputs:
- grad_image_feats: bfloat16 [131072, 1152], P(('blk', 'rep'))
- grad_text_feats: bfloat16 [131072, 1152], P(('blk', 'rep'))
- grad_head: float32 [1152, 1152], P('blk')
Inputs may be any that keep to these rules, and one draw needn't show every extreme that they name: `image_feats`: row magnitudes differ from row to row. `text_feats`: row magnitudes differ from row to row.
All inputs are finite; a program needn't handle non-finite values.
Results may differ from a plain program's by a relative error of at most 0.0072.
Values may be sent and summed in bfloat16 or wider, within the bound.
No kernel may reach another device: no remote copies, remote signals or barrier semaphores. Data moves between devices by JAX's collectives and lax.ppermute only.
A program may use at most 128 MiB of HBM per device.

v0:
```python
import jax
import jax.numpy as jnp
from jax import lax
from jax.sharding import PartitionSpec as P

HOPS = 4


def shifted(value, axis, steps):
    count = lax.axis_size(axis)
    pairs = [(source, (source + steps) % count) for source in range(count)]
    return lax.ppermute(value, axis, pairs)


def unit_rows(values):
    inverse = lax.rsqrt(jnp.sum(values * values, axis=-1, keepdims=True) + 1e-06)
    return (values * inverse, inverse)


def per_device(image_feats, text_feats, head, image_ids, text_ids, log_scale, bias):
    u_local = jnp.dot(image_feats, head, preferred_element_type=jnp.float32)
    x_full, inv_u = unit_rows(u_local)
    x_half = x_full.astype(jnp.bfloat16)
    y_full, inv_t = unit_rows(text_feats.astype(jnp.float32))
    y_half = y_full.astype(jnp.bfloat16)
    scale = jnp.exp(log_scale[0])
    offset = bias[0]

    def coefficients(images, image_labels, texts, text_labels):
        logits = (
            scale * jnp.einsum("id,jd->ij", images, texts, preferred_element_type=jnp.float32)
            + offset
        )
        positive = (image_labels[:, None] == text_labels[None, :]).astype(jnp.float32)
        return (scale * (jax.nn.sigmoid(logits) - positive)).astype(jnp.bfloat16)

    def tile(block, block_ids):
        coef = coefficients(x_half, image_ids, block, block_ids)
        image_part = jnp.dot(coef, block, preferred_element_type=jnp.float32)
        text_part = jnp.einsum("ij,id->jd", coef, x_half, preferred_element_type=jnp.float32)
        return (image_part, text_part)

    grad_x, text_sum = tile(y_half, text_ids)
    block, block_ids = (y_half, text_ids)
    for hop in range(1, HOPS + 1):
        block = shifted(block, "blk", 1)
        block_ids = shifted(block_ids, "blk", 1)
        image_part, text_part = tile(block, block_ids)
        grad_x = grad_x + image_part
        text_sum = shifted(text_sum, "blk", 1) + text_part
    grad_y = shifted(text_sum, "blk", -HOPS)
    grad_u = (inv_u * (grad_x - x_full * jnp.sum(x_full * grad_x, axis=1, keepdims=True))).astype(
        jnp.bfloat16
    )
    grad_image = jnp.einsum("id,ed->ie", grad_u, head, preferred_element_type=jnp.float32).astype(
        jnp.bfloat16
    )
    cycle_rows = lax.psum_scatter(
        jnp.einsum("ie,id->ed", image_feats, grad_u, preferred_element_type=jnp.float32),
        "blk",
        scatter_dimension=0,
        tiled=True,
    )
    devices_all = lax.axis_size("blk") * lax.axis_size("rep")
    grad_head = lax.psum(cycle_rows, "rep") / devices_all
    grad_text = (
        inv_t * (grad_y - y_full * jnp.sum(y_full * grad_y, axis=1, keepdims=True))
    ).astype(jnp.bfloat16)
    return (grad_image, grad_text, grad_head)


def solution(mesh):
    placed = (
        P(("blk", "rep"), None),
        P(("blk", "rep"), None),
        P(),
        P(("blk", "rep")),
        P(("blk", "rep")),
        P(),
        P(),
    )
    return jax.shard_map(
        per_device,
        mesh=mesh,
        in_specs=placed,
        out_specs=(P(("blk", "rep"), None), P(("blk", "rep"), None), P("blk", None)),
        check_vma=False,
    )
```

profile of v0, /device:TPU:1, one launch (start us, length us, event | category | flops | bytes accessed | tf_op | source)
XLA Modules:
  0.0 1003.0 jit_solution(10093257569630580109)
XLA Ops:
  7.2 0.0 copy-start
  7.2 0.0 all-reduce.6.cloned.1.call-start
  7.2 0.0 copy-start.3
  7.2 1.7 fusion.7
  9.0 0.0 copy-done.3
  9.0 0.3 fusion.2
  9.3 2.5 collective-permute-start
  11.8 2.0 multiply_reduce_fusion.1
  15.1 0.0 copy-start.9
  15.2 0.0 copy-start.10
  15.2 0.2 multiply_convert_fusion.1
  15.4 0.0 copy-start.1
  15.4 0.4 copy-done.9
  15.8 0.0 copy-done.10
  15.8 1.1 fusion.43
  16.9 0.9 fusion.49
  17.8 1.7 collective-permute-start.8
  19.5 25.3 %collective-permute-done = bf16[512,1152]{1,0:T(8,128)(2,1)S(1)} collective-permute-done((bf16[512,1152]{1,0:T(8,128)(2,1)S(1)}, bf16[512,1152]{1,0:T(8,128)(2,1)S(1)}, u32[]{:S(2)}, u32[]{:S(2)}) %collective-permute-start) | collective-permute-done | bytes 1179680 | tf_op jit(solution)/shard_map/ppermute | solution.py:12
  44.8 0.0 collective-permute-start.2
  44.8 75.9 %collective-permute-done.1 = s32[512]{0:T(512)S(1)} collective-permute-done((s32[512]{0:T(512)S(1)}, s32[512]{0:T(512)S(1)}, u32[]{:S(2)}, u32[]{:S(2)}) %collective-permute-start.1) | collective-permute-done | bytes 2080 | tf_op jit(solution)/shard_map/ppermute | solution.py:12
  120.7 6.7 collective-permute-done.3
  127.4 1.1 fusion.44
  128.5 0.1 collective-permute-start.4
  128.6 0.9 convolution_add_fusion
  129.5 0.3 collective-permute-start.9
  129.7 0.8 fusion.48
  130.6 3.4 collective-permute-done.5
  134.0 0.9 convolution_add_fusion.4
  134.9 1.1 fusion.45
  136.0 21.9 %collective-permute-done.4 = bf16[512,1152]{1,0:T(8,128)(2,1)S(1)} collective-permute-done((bf16[512,1152]{1,0:T(8,128)(2,1)S(1)}, bf16[512,1152]{1,0:T(8,128)(2,1)S(1)}, u32[]{:S(2)}, u32[]{:S(2)}) %collective-permute-start.4) | collective-permute-done | bytes 1179680 | tf_op jit(solution)/shard_map/ppermute | solution.py:12
  157.9 0.9 fusion.50
  158.8 0.9 convolution_add_fusion.3
  159.6 1.1 fusion.46
  160.7 0.9 convolution_add_fusion.2
  161.6 46.8 %collective-permute-done.9 = f32[512,1152]{1,0:T(8,128)S(1)} collective-permute-done((f32[512,1152]{1,0:T(8,128)S(1)}, f32[512,1152]{1,0:T(8,128)S(1)}, u32[]{:S(2)}, u32[]{:S(2)}) %collective-permute-start.9) | collective-permute-done | bytes 2359328 | tf_op jit(solution)/shard_map/ppermute | solution.py:12
  208.5 1.7 add.99
  210.2 23.6 %collective-permute-done.6 = bf16[512,1152]{1,0:T(8,128)(2,1)S(1)} collective-permute-done((bf16[512,1152]{1,0:T(8,128)(2,1)S(1)}, bf16[512,1152]{1,0:T(8,128)(2,1)S(1)}, u32[]{:S(2)}, u32[]{:S(2)}) %collective-permute-start.6) | collective-permute-done | bytes 1179680 | tf_op jit(solution)/shard_map/ppermute | solution.py:12
  233.8 1.1 fusion.47
  234.9 1.1 multiply_reduce_fusion
  236.0 0.4 multiply_convert_fusion
  236.4 0.0 copy-start.5
  236.4 1.0 copy-done.5
  237.4 4.1 convolution_bitcast_fusion
  241.6 0.0 all-reduce.6.cloned.1.call-update
  241.6 0.0 all-reduce.4.cloned.1.call-start
  241.6 2.1 fusion.51
  243.8 0.0 copy-start.2
  243.8 47.0 %collective-permute-done.10 = f32[512,1152]{1,0:T(8,128)} collective-permute-done((f32[512,1152]{1,0:T(8,128)}, f32[512,1152]{1,0:T(8,128)}, u32[]{:S(2)}, u32[]{:S(2)}) %collective-permute-start.10) | collective-permute-done | bytes 2359328 | tf_op jit(solution)/shard_map/ppermute | solution.py:12
  290.8 2.0 add.100
  292.8 0.3 collective-permute-start.11
  293.1 0.9 fusion.52
  294.0 0.0 copy-start.11
  294.0 65.8 %collective-permute-done.11 = f32[512,1152]{1,0:T(8,128)S(1)} collective-permute-done((f32[512,1152]{1,0:T(8,128)S(1)}, f32[512,1152]{1,0:T(8,128)S(1)}, u32[]{:S(2)}, u32[]{:S(2)}) %collective-permute-start.11) | collective-permute-done | bytes 2359328 | tf_op jit(solution)/shard_map/ppermute | solution.py:12
  359.8 1.7 add.101
  361.5 0.6 dynamic-slice
  362.8 539.7 %all-reduce.6.cloned.1.call-done = f32[1152,1152]{0,1:T(8,128)} async-done(((f32[1152,1152]{0,1:T(8,128)}), f32[1152,1152]{0,1:T(8,128)}) %all-reduce.6.cloned.1.call-update) | async-done | bytes 5308432
  902.5 2.3 constant_dynamic-slice_fusion
  904.8 0.0 all-reduce.4.cloned.1.call-update
  904.8 4.1 convolution_convert_fusion
  909.0 79.4 %all-reduce.4.cloned.1.call-done = f32[18,1152]{0,1:T(8,128)} async-done(((f32[18,1152]{0,1:T(8,128)}), f32[18,1152]{0,1:T(8,128)}) %all-reduce.4.cloned.1.call-update) | async-done | bytes 82960 | tf_op jit(solution)/shard_map/psum | solution.py:65
  988.4 1.1 broadcast_multiply_fusion
  989.6 0.9 copy.11
  990.4 2.5 fusion.3
  993.0 3.2 fusion.6
  (25 shorter events, 0.1 us)
Async XLA Ops:
  7.2 4.7 copy-start
  7.2 895.3 %all-reduce.6.cloned.1.call-start = ((), (), s32[]{:S(2)}) async-start(), calls=%async_computation.1 | async-start | bytes 10616832
  7.2 1.8 copy-start.3
  9.0 2.8 copy-start.8
  9.3 35.6 %collective-permute-start = (bf16[512,1152]{1,0:T(8,128)(2,1)S(1)}, bf16[512,1152]{1,0:T(8,128)(2,1)S(1)}, u32[]{:S(2)}, u32[]{:S(2)}) collective-permute-start(bf16[512,1152]{1,0:T(8,128)(2,1)S(1)} %fusion.2), channel_id=1, source_target_pairs={{0,4},{4,8},{8,12},{12,16},{16,20},{20,24},{24,28},{28,32},{32,36}... | collective-permute-start | bytes 3538952 | tf_op jit(solution)/shard_map/ppermute | solution.py:12
  15.1 0.7 copy-start.9
  15.2 0.7 copy-start.10
  15.4 218.4 %copy-start.1 = (bf16[512,1152]{1,0:T(8,128)(2,1)}, bf16[512,1152]{1,0:T(8,128)(2,1)S(1)}, u32[]{:S(2)}) copy-start(bf16[512,1152]{1,0:T(8,128)(2,1)S(1)} %multiply_convert_fusion.1) | copy-start | bytes 3538948
  17.8 110.7 %collective-permute-start.8 = (f32[512,1152]{1,0:T(8,128)S(1)}, f32[512,1152]{1,0:T(8,128)S(1)}, u32[]{:S(2)}, u32[]{:S(2)}) collective-permute-start(f32[512,1152]{1,0:T(8,128)S(1)} %fusion.49), channel_id=1, source_target_pairs={{0,4},{4,8},{8,12},{12,16},{16,20},{20,24},{24,28},{28,32},{32,36}... | collective-permute-start | bytes 7077896 | tf_op jit(solution)/shard_map/ppermute | solution.py:12
  44.8 83.6 %collective-permute-start.2 = (bf16[512,1152]{1,0:T(8,128)(2,1)S(1)}, bf16[512,1152]{1,0:T(8,128)(2,1)S(1)}, u32[]{:S(2)}, u32[]{:S(2)}) collective-permute-start(bf16[512,1152]{1,0:T(8,128)(2,1)S(1)} %collective-permute-done), channel_id=1, source_target_pairs={{0,4},{4,8},{8,12},{12,16},{16,20},{20,24},{24,28},{28,32},{32,36}... | collective-permute-start | bytes 3538952 | tf_op jit(solution)/shard_map/ppermute | solution.py:12
  44.8 75.9 %collective-permute-start.1 = (s32[512]{0:T(512)S(1)}, s32[512]{0:T(512)S(1)}, u32[]{:S(2)}, u32[]{:S(2)}) collective-permute-start(s32[512]{0:T(512)S(1)} %copy-done.9), channel_id=1, source_target_pairs={{0,4},{4,8},{8,12},{12,16},{16,20},{20,24},{24,28},{28,32},{32,36}... | collective-permute-start | bytes 6152 | tf_op jit(solution)/shard_map/ppermute | solution.py:12
  120.7 6.7 collective-permute-start.3
  127.4 6.7 collective-permute-start.5
  128.5 29.4 %collective-permute-start.4 = (bf16[512,1152]{1,0:T(8,128)(2,1)S(1)}, bf16[512,1152]{1,0:T(8,128)(2,1)S(1)}, u32[]{:S(2)}, u32[]{:S(2)}) collective-permute-start(bf16[512,1152]{1,0:T(8,128)(2,1)S(1)} %collective-permute-done.2), channel_id=1, source_target_pairs={{0,4},{4,8},{8,12},{12,16},{16,20},{20,24},{24,28},{28,32},{32,36}... | collective-permute-start | bytes 3538952 | tf_op jit(solution)/shard_map/ppermute | solution.py:12
  129.5 79.0 %collective-permute-start.9 = (f32[512,1152]{1,0:T(8,128)S(1)}, f32[512,1152]{1,0:T(8,128)S(1)}, u32[]{:S(2)}, u32[]{:S(2)}) collective-permute-start(f32[512,1152]{1,0:T(8,128)S(1)} %convolution_add_fusion), channel_id=1, source_target_pairs={{0,4},{4,8},{8,12},{12,16},{16,20},{20,24},{24,28},{28,32},{32,36}... | collective-permute-start | bytes 7077896 | tf_op jit(solution)/shard_map/ppermute | solution.py:12
  134.0 76.1 %collective-permute-start.7 = (s32[512]{0:T(512)S(1)}, s32[512]{0:T(512)S(1)}, u32[]{:S(2)}, u32[]{:S(2)}) collective-permute-start(s32[512]{0:T(512)S(1)} %collective-permute-done.5), channel_id=1, source_target_pairs={{0,4},{4,8},{8,12},{12,16},{16,20},{20,24},{24,28},{28,32},{32,36}... | collective-permute-start | bytes 6152 | tf_op jit(solution)/shard_map/ppermute | solution.py:12
  157.9 75.9 %collective-permute-start.6 = (bf16[512,1152]{1,0:T(8,128)(2,1)S(1)}, bf16[512,1152]{1,0:T(8,128)(2,1)S(1)}, u32[]{:S(2)}, u32[]{:S(2)}) collective-permute-start(bf16[512,1152]{1,0:T(8,128)(2,1)S(1)} %collective-permute-done.4), channel_id=1, source_target_pairs={{0,4},{4,8},{8,12},{12,16},{16,20},{20,24},{24,28},{28,32},{32,36}... | collective-permute-start | bytes 3538952 | tf_op jit(solution)/shard_map/ppermute | solution.py:12
  210.2 80.6 %collective-permute-start.10 = (f32[512,1152]{1,0:T(8,128)}, f32[512,1152]{1,0:T(8,128)}, u32[]{:S(2)}, u32[]{:S(2)}) collective-permute-start(f32[512,1152]{1,0:T(8,128)} %add.99), channel_id=1, source_target_pairs={{0,4},{4,8},{8,12},{12,16},{16,20},{20,24},{24,28},{28,32},{32,36}... | collective-permute-start | bytes 7077896 | tf_op jit(solution)/shard_map/ppermute | solution.py:12
  234.9 1.1 copy-start.6
  236.4 1.0 copy-start.5
  241.6 746.9 %all-reduce.4.cloned.1.call-start = ((), (), s32[]{:S(2)}) async-start(), calls=%async_computation | async-start | bytes 1179648 | tf_op jit(solution)/shard_map/psum | solution.py:65
  243.8 49.3 %copy-start.2 = (bf16[512,1152]{1,0:T(8,128)(2,1)S(1)}, bf16[512,1152]{1,0:T(8,128)(2,1)}, u32[]{:S(2)}) copy-start(bf16[512,1152]{1,0:T(8,128)(2,1)} %copy-done.1) | copy-start | bytes 3538948
  243.8 49.3 %copy-start.7 = (bf16[512,512]{1,0:T(8,128)(2,1)S(1)}, bf16[512,512]{1,0:T(8,128)(2,1)}, u32[]{:S(2)}) copy-start(bf16[512,512]{1,0:T(8,128)(2,1)} %copy-done.6) | copy-start | bytes 1572868
  292.8 67.1 %collective-permute-start.11 = (f32[512,1152]{1,0:T(8,128)S(1)}, f32[512,1152]{1,0:T(8,128)S(1)}, u32[]{:S(2)}, u32[]{:S(2)}) collective-permute-start(f32[512,1152]{1,0:T(8,128)S(1)} %add.100), channel_id=1, source_target_pairs={{0,4},{4,8},{8,12},{12,16},{16,20},{20,24},{24,28},{28,32},{32,36}... | collective-permute-start | bytes 7077896 | tf_op jit(solution)/shard_map/ppermute | solution.py:12
  294.0 67.6 %copy-start.11 = (u32[256]{0:T(256)S(1)}, u32[256]{0:T(256)}, u32[]{:S(2)}) copy-start(u32[256]{0:T(256)} %constant.11) | copy-start | bytes 3076
  361.5 628.9 %collective-permute-start.12 = (f32[512,1152]{1,0:T(8,128)}, f32[512,1152]{1,0:T(8,128)}, u32[]{:S(2)}, u32[]{:S(2)}) collective-permute-start(f32[512,1152]{1,0:T(8,128)} %add.101), channel_id=1, source_target_pairs={{0,240},{4,244},{8,248},{12,252},{16,0},{20,4},{24,8},{28,12},{32,... | collective-permute-start | bytes 7077896 | tf_op jit(solution)/shard_map/ppermute | solution.py:12
  990.4 2.5 copy-start.4
Sparse Core Ops, SparseCore 0:
  241.7 660.7 all-reduce.5
  905.1 83.2 all-reduce.3
where the time goes:
time: 1000 us
  waiting for transfers between devices  936 us (94%)
  matrix products  25.8 us (3%)
  between operations  16.3 us (2%)
  other arithmetic  14.8 us (1%)
    unnamed x3, waiting for transfers between devices  540 us
    ppermute x13, waiting for transfers between devices, shifted(): return lax.ppermute(value, axis, pairs)  316 us
    psum x1, waiting for transfers between devices, per_device(): grad_head = lax.psum(cycle_rows, 'rep') / devices_all  79.4 us
  transfers between devices with their start and end apart: 15, of which 11 were waited for; matrix products, arithmetic and copies ran while one was open for 4% of the time, Pallas kernels for 0%

commit v1 on v0

--- a/solution.py
+++ b/solution.py
@@ -62,7 +62,7 @@
         tiled=True,
     )
     devices_all = lax.axis_size("blk") * lax.axis_size("rep")
-    grad_head = lax.psum(cycle_rows, "rep") / devices_all
+    grad_head = jnp.sum(lax.all_gather(cycle_rows, "rep"), axis=0) / devices_all
     grad_text = (
         inv_t * (grad_y - y_full * jnp.sum(y_full * grad_y, axis=1, keepdims=True))
     ).astype(jnp.bfloat16)

time: 1000 us -> 968 us (0.968)
  waiting for transfers between devices: 936 us -> 852 us
  blocking collectives: 0 us -> 48.2 us
    psum x1 -> x0, waiting for transfers between devices: 79.4 us -> none  [per_device(): grad_head = lax.psum(cycle_rows, 'rep') / devices_all]
    all_gather x0 -> x1, blocking collectives: none -> 48.2 us  [per_device(): grad_head = jnp.sum(lax.all_gather(cycle_rows, 'rep'), axis=0) / devices_all]
    unnamed x3 -> x2, waiting for transfers between devices: 540 us -> 535 us
  transfers between devices with their start and end apart: 15 -> 14, of which waited for: 11 -> 10; matrix products, arithmetic and copies ran while one was open for 4% -> 4% of each run, Pallas kernels for 0% -> 0%
where the time goes in v1:
time: 968 us
  waiting for transfers between devices  852 us (88%)
  blocking collectives  48.2 us (5%)
  matrix products  25.8 us (3%)
  between operations  16.3 us (2%)
  other arithmetic  14.6 us (2%)
    unnamed x2, waiting for transfers between devices  535 us
    ppermute x13, waiting for transfers between devices, shifted(): return lax.ppermute(value, axis, pairs)  317 us
    all_gather x1, blocking collectives, per_device(): grad_head = jnp.sum(lax.all_gather(cycle_rows, 'rep'), axis=0) / devices_all  48.2 us
  transfers between devices with their start and end apart: 14, of which 10 were waited for; matrix products, arithmetic and copies ran while one was open for 4% of the time, Pallas kernels for 0%

profile of v1, /device:TPU:1, one launch (start us, length us, event | category | flops | bytes accessed | tf_op | source)
XLA Modules:
  0.0 968.0 jit_solution(9709102906618435654)
XLA Ops:
  7.2 0.0 copy-start
  7.2 0.0 all-reduce.3.cloned.1.call-start
  7.2 0.0 copy-start.3
  7.2 1.7 fusion.7
  9.0 0.0 copy-done.3
  9.0 0.3 fusion.2
  9.3 2.5 collective-permute-start
  11.8 2.0 multiply_reduce_fusion.1
  15.1 0.0 copy-start.9
  15.2 0.0 copy-start.10
  15.2 0.2 multiply_convert_fusion.1
  15.4 0.0 copy-start.1
  15.4 0.4 copy-done.9
  15.8 0.0 copy-done.10
  15.8 1.1 fusion.43
  16.9 0.9 fusion.49
  17.8 1.7 collective-permute-start.8
  19.5 25.3 %collective-permute-done = bf16[512,1152]{1,0:T(8,128)(2,1)S(1)} collective-permute-done((bf16[512,1152]{1,0:T(8,128)(2,1)S(1)}, bf16[512,1152]{1,0:T(8,128)(2,1)S(1)}, u32[]{:S(2)}, u32[]{:S(2)}) %collective-permute-start) | collective-permute-done | bytes 1179680 | tf_op jit(solution)/shard_map/ppermute | solution.py:12
  44.8 0.0 collective-permute-start.2
  44.8 75.9 %collective-permute-done.1 = s32[512]{0:T(512)S(1)} collective-permute-done((s32[512]{0:T(512)S(1)}, s32[512]{0:T(512)S(1)}, u32[]{:S(2)}, u32[]{:S(2)}) %collective-permute-start.1) | collective-permute-done | bytes 2080 | tf_op jit(solution)/shard_map/ppermute | solution.py:12
  120.7 6.7 collective-permute-done.3
  127.4 1.1 fusion.44
  128.5 0.1 collective-permute-start.4
  128.6 0.9 convolution_add_fusion
  129.5 0.3 collective-permute-start.9
  129.7 0.8 fusion.48
  130.6 3.4 collective-permute-done.5
  134.0 0.9 convolution_add_fusion.4
  134.9 1.1 fusion.45
  136.0 21.9 %collective-permute-done.4 = bf16[512,1152]{1,0:T(8,128)(2,1)S(1)} collective-permute-done((bf16[512,1152]{1,0:T(8,128)(2,1)S(1)}, bf16[512,1152]{1,0:T(8,128)(2,1)S(1)}, u32[]{:S(2)}, u32[]{:S(2)}) %collective-permute-start.4) | collective-permute-done | bytes 1179680 | tf_op jit(solution)/shard_map/ppermute | solution.py:12
  157.9 0.9 fusion.50
  158.8 0.8 convolution_add_fusion.3
  159.6 1.1 fusion.46
  160.7 0.9 convolution_add_fusion.2
  161.6 46.8 %collective-permute-done.9 = f32[512,1152]{1,0:T(8,128)S(1)} collective-permute-done((f32[512,1152]{1,0:T(8,128)S(1)}, f32[512,1152]{1,0:T(8,128)S(1)}, u32[]{:S(2)}, u32[]{:S(2)}) %collective-permute-start.9) | collective-permute-done | bytes 2359328 | tf_op jit(solution)/shard_map/ppermute | solution.py:12
  208.5 1.7 add.97
  210.2 23.6 %collective-permute-done.6 = bf16[512,1152]{1,0:T(8,128)(2,1)S(1)} collective-permute-done((bf16[512,1152]{1,0:T(8,128)(2,1)S(1)}, bf16[512,1152]{1,0:T(8,128)(2,1)S(1)}, u32[]{:S(2)}, u32[]{:S(2)}) %collective-permute-start.6) | collective-permute-done | bytes 1179680 | tf_op jit(solution)/shard_map/ppermute | solution.py:12
  233.8 1.1 fusion.47
  234.9 1.1 multiply_reduce_fusion
  236.0 0.4 multiply_convert_fusion
  236.4 0.0 copy-start.5
  236.4 1.0 copy-done.5
  237.4 4.1 convolution_bitcast_fusion
  241.5 0.0 all-reduce.3.cloned.1.call-update
  241.6 2.1 fusion.51
  243.7 0.0 copy-start.2
  243.7 47.0 %collective-permute-done.10 = f32[512,1152]{1,0:T(8,128)} collective-permute-done((f32[512,1152]{1,0:T(8,128)}, f32[512,1152]{1,0:T(8,128)}, u32[]{:S(2)}, u32[]{:S(2)}) %collective-permute-start.10) | collective-permute-done | bytes 2359328 | tf_op jit(solution)/shard_map/ppermute | solution.py:12
  290.8 2.0 add.98
  292.8 0.3 collective-permute-start.11
  293.1 0.9 fusion.52
  294.0 0.0 copy-start.11
  294.0 66.1 %collective-permute-done.11 = f32[512,1152]{1,0:T(8,128)S(1)} collective-permute-done((f32[512,1152]{1,0:T(8,128)S(1)}, f32[512,1152]{1,0:T(8,128)S(1)}, u32[]{:S(2)}, u32[]{:S(2)}) %collective-permute-start.11) | collective-permute-done | bytes 2359328 | tf_op jit(solution)/shard_map/ppermute | solution.py:12
  360.1 1.7 add.99
  361.8 0.6 dynamic-slice
  363.0 4.2 convolution_convert_fusion
  367.2 535.3 %all-reduce.3.cloned.1.call-done = f32[1152,1152]{0,1:T(8,128)} async-done(((f32[1152,1152]{0,1:T(8,128)}), f32[1152,1152]{0,1:T(8,128)}) %all-reduce.3.cloned.1.call-update) | async-done | bytes 5308432
  902.5 1.5 dynamic-slice_bitcast_fusion
  904.0 0.2 copy.10
  904.2 48.2 %all-gather.1 = f32[4,18,1152]{2,1,0:T(8,128)S(1)} all-gather(f32[1,18,1152]{2,1,0:T(8,128)S(1)} %copy.10), channel_id=2, replica_groups=mesh['blk'=64,'rep'=4] {'rep'}, dimensions={0}, use_global_device_ids=true | all-gather | bytes 414720 | tf_op jit(solution)/shard_map/all_gather | solution.py:65
  952.4 0.2 copy.15
  952.6 0.9 broadcast_multiply_fusion
  953.5 1.9 copy.12
  955.4 2.5 fusion.3
  958.0 3.2 fusion.6
  (26 shorter events, 0.1 us)
Async XLA Ops:
  7.2 4.7 copy-start
  7.2 895.3 %all-reduce.3.cloned.1.call-start = ((), (), s32[]{:S(2)}) async-start(), calls=%async_computation | async-start | bytes 10616832
  7.2 1.8 copy-start.3
  9.0 2.8 copy-start.8
  9.3 35.6 %collective-permute-start = (bf16[512,1152]{1,0:T(8,128)(2,1)S(1)}, bf16[512,1152]{1,0:T(8,128)(2,1)S(1)}, u32[]{:S(2)}, u32[]{:S(2)}) collective-permute-start(bf16[512,1152]{1,0:T(8,128)(2,1)S(1)} %fusion.2), channel_id=1, source_target_pairs={{0,4},{4,8},{8,12},{12,16},{16,20},{20,24},{24,28},{28,32},{32,36}... | collective-permute-start | bytes 3538952 | tf_op jit(solution)/shard_map/ppermute | solution.py:12
  15.1 0.7 copy-start.9
  15.2 0.7 copy-start.10
  15.4 218.4 %copy-start.1 = (bf16[512,1152]{1,0:T(8,128)(2,1)}, bf16[512,1152]{1,0:T(8,128)(2,1)S(1)}, u32[]{:S(2)}) copy-start(bf16[512,1152]{1,0:T(8,128)(2,1)S(1)} %multiply_convert_fusion.1) | copy-start | bytes 3538948
  17.8 110.7 %collective-permute-start.8 = (f32[512,1152]{1,0:T(8,128)S(1)}, f32[512,1152]{1,0:T(8,128)S(1)}, u32[]{:S(2)}, u32[]{:S(2)}) collective-permute-start(f32[512,1152]{1,0:T(8,128)S(1)} %fusion.49), channel_id=1, source_target_pairs={{0,4},{4,8},{8,12},{12,16},{16,20},{20,24},{24,28},{28,32},{32,36}... | collective-permute-start | bytes 7077896 | tf_op jit(solution)/shard_map/ppermute | solution.py:12
  44.8 83.6 %collective-permute-start.2 = (bf16[512,1152]{1,0:T(8,128)(2,1)S(1)}, bf16[512,1152]{1,0:T(8,128)(2,1)S(1)}, u32[]{:S(2)}, u32[]{:S(2)}) collective-permute-start(bf16[512,1152]{1,0:T(8,128)(2,1)S(1)} %collective-permute-done), channel_id=1, source_target_pairs={{0,4},{4,8},{8,12},{12,16},{16,20},{20,24},{24,28},{28,32},{32,36}... | collective-permute-start | bytes 3538952 | tf_op jit(solution)/shard_map/ppermute | solution.py:12
  44.8 75.9 %collective-permute-start.1 = (s32[512]{0:T(512)S(1)}, s32[512]{0:T(512)S(1)}, u32[]{:S(2)}, u32[]{:S(2)}) collective-permute-start(s32[512]{0:T(512)S(1)} %copy-done.9), channel_id=1, source_target_pairs={{0,4},{4,8},{8,12},{12,16},{16,20},{20,24},{24,28},{28,32},{32,36}... | collective-permute-start | bytes 6152 | tf_op jit(solution)/shard_map/ppermute | solution.py:12
  120.7 6.7 collective-permute-start.3
  127.4 6.7 collective-permute-start.5
  128.5 29.4 %collective-permute-start.4 = (bf16[512,1152]{1,0:T(8,128)(2,1)S(1)}, bf16[512,1152]{1,0:T(8,128)(2,1)S(1)}, u32[]{:S(2)}, u32[]{:S(2)}) collective-permute-start(bf16[512,1152]{1,0:T(8,128)(2,1)S(1)} %collective-permute-done.2), channel_id=1, source_target_pairs={{0,4},{4,8},{8,12},{12,16},{16,20},{20,24},{24,28},{28,32},{32,36}... | collective-permute-start | bytes 3538952 | tf_op jit(solution)/shard_map/ppermute | solution.py:12
  129.5 79.0 %collective-permute-start.9 = (f32[512,1152]{1,0:T(8,128)S(1)}, f32[512,1152]{1,0:T(8,128)S(1)}, u32[]{:S(2)}, u32[]{:S(2)}) collective-permute-start(f32[512,1152]{1,0:T(8,128)S(1)} %convolution_add_fusion), channel_id=1, source_target_pairs={{0,4},{4,8},{8,12},{12,16},{16,20},{20,24},{24,28},{28,32},{32,36}... | collective-permute-start | bytes 7077896 | tf_op jit(solution)/shard_map/ppermute | solution.py:12
  134.0 76.1 %collective-permute-start.7 = (s32[512]{0:T(512)S(1)}, s32[512]{0:T(512)S(1)}, u32[]{:S(2)}, u32[]{:S(2)}) collective-permute-start(s32[512]{0:T(512)S(1)} %collective-permute-done.5), channel_id=1, source_target_pairs={{0,4},{4,8},{8,12},{12,16},{16,20},{20,24},{24,28},{28,32},{32,36}... | collective-permute-start | bytes 6152 | tf_op jit(solution)/shard_map/ppermute | solution.py:12
  157.9 75.9 %collective-permute-start.6 = (bf16[512,1152]{1,0:T(8,128)(2,1)S(1)}, bf16[512,1152]{1,0:T(8,128)(2,1)S(1)}, u32[]{:S(2)}, u32[]{:S(2)}) collective-permute-start(bf16[512,1152]{1,0:T(8,128)(2,1)S(1)} %collective-permute-done.4), channel_id=1, source_target_pairs={{0,4},{4,8},{8,12},{12,16},{16,20},{20,24},{24,28},{28,32},{32,36}... | collective-permute-start | bytes 3538952 | tf_op jit(solution)/shard_map/ppermute | solution.py:12
  210.1 80.6 %collective-permute-start.10 = (f32[512,1152]{1,0:T(8,128)}, f32[512,1152]{1,0:T(8,128)}, u32[]{:S(2)}, u32[]{:S(2)}) collective-permute-start(f32[512,1152]{1,0:T(8,128)} %add.97), channel_id=1, source_target_pairs={{0,4},{4,8},{8,12},{12,16},{16,20},{20,24},{24,28},{28,32},{32,36}... | collective-permute-start | bytes 7077896 | tf_op jit(solution)/shard_map/ppermute | solution.py:12
  234.9 1.1 copy-start.6
  236.4 1.0 copy-start.5
  243.7 49.4 %copy-start.2 = (bf16[512,1152]{1,0:T(8,128)(2,1)S(1)}, bf16[512,1152]{1,0:T(8,128)(2,1)}, u32[]{:S(2)}) copy-start(bf16[512,1152]{1,0:T(8,128)(2,1)} %copy-done.1) | copy-start | bytes 3538948
  243.7 49.4 %copy-start.7 = (bf16[512,512]{1,0:T(8,128)(2,1)S(1)}, bf16[512,512]{1,0:T(8,128)(2,1)}, u32[]{:S(2)}) copy-start(bf16[512,512]{1,0:T(8,128)(2,1)} %copy-done.6) | copy-start | bytes 1572868
  292.8 67.3 %collective-permute-start.11 = (f32[512,1152]{1,0:T(8,128)S(1)}, f32[512,1152]{1,0:T(8,128)S(1)}, u32[]{:S(2)}, u32[]{:S(2)}) collective-permute-start(f32[512,1152]{1,0:T(8,128)S(1)} %add.98), channel_id=1, source_target_pairs={{0,4},{4,8},{8,12},{12,16},{16,20},{20,24},{24,28},{28,32},{32,36}... | collective-permute-start | bytes 7077896 | tf_op jit(solution)/shard_map/ppermute | solution.py:12
  294.0 67.8 %copy-start.11 = (u32[256]{0:T(256)S(1)}, u32[256]{0:T(256)}, u32[]{:S(2)}) copy-start(u32[256]{0:T(256)} %constant.11) | copy-start | bytes 3076
  361.8 593.7 %collective-permute-start.12 = (f32[512,1152]{1,0:T(8,128)}, f32[512,1152]{1,0:T(8,128)}, u32[]{:S(2)}, u32[]{:S(2)}) collective-permute-start(f32[512,1152]{1,0:T(8,128)} %add.99), channel_id=1, source_target_pairs={{0,240},{4,244},{8,248},{12,252},{16,0},{20,4},{24,8},{28,12},{32,... | collective-permute-start | bytes 7077896 | tf_op jit(solution)/shard_map/ppermute | solution.py:12
  955.4 2.5 copy-start.4
Sparse Core Ops, SparseCore 0:
  241.7 660.7 all-reduce.2
